TPU v7x, 512 devices: a whole 4x8x8 slice. The times are simulated.
512 devices in a mesh: rep: 16 (over y, core), tp: 8 (over x, z_lo), fsdp: 4 (over z_hi).
Axes of the slice: x: 4, y: 8, z: 8 (z_hi: 4, z_lo: 2; z = z_hi * 2 + z_lo), core: 2. Of those that a mesh axis runs over, the one named last changes fastest.
Arguments:
- hidden_in: bfloat16 [65536, 5120], P(('rep', 'fsdp'), 'tp'), may hold values from -6 to 6
- target_rows: bfloat16 [65536, 5120], P(('rep', 'fsdp'), 'tp'), may hold values from -0.078125 to 0.078125
- grads: float32 [5120, 5120], P(('rep', 'fsdp'), 'tp')
- master: float32 [5120, 5120], P(('rep', 'fsdp'), 'tp'), may hold values from -0.078125 to 0.078125
- first_moment: float32 [5120, 5120], P(('rep', 'fsdp'), 'tp'), may hold values from -0.0012 to 0.0012
- second_moment: float32 [5120, 5120], P(('rep', 'fsdp'), 'tp'), may hold values from 1e-09 to 1e-07
- ref_weight: bfloat16 [5120, 5120], P(('rep', 'fsdp'), 'tp'), may hold values from -0.078125 to 0.078125
- lengths: int32 [64], P(('rep', 'fsdp')), may hold values from 768 to 1024, as said below
- boundaries: int32 [64, 8], P(('rep', 'fsdp')), may hold values from 1 to 1023, as said below
Outputs:
- step_rewards: float32 [64, 9], P(('rep', 'fsdp'))
- master_new: float32 [5120, 5120], P(('rep', 'fsdp'), 'tp')
- moment_one: float32 [5120, 5120], P(('rep', 'fsdp'), 'tp')
- moment_two: float32 [5120, 5120], P(('rep', 'fsdp'), 'tp')
Inputs may be any that keep to these rules, and one draw needn't show every extreme that they name: lengths lie between 768 and 1024; some rollout has length 1024. boundaries of a rollout rise strictly and stay below its length.
All inputs are finite; a program needn't handle non-finite values.
Results may differ from a plain program's by a relative error of at most 0.0031.
Values may be sent and summed in bfloat16 or wider, within the bound.
A program may use at most 64 MiB of HBM per device.

v0:
```python
import jax
import jax.numpy as jnp
from jax import lax
from jax.sharding import PartitionSpec as P

STEPS = 8


first_fix = 1.0 - (0.9**10) ** 10
second_fix = 1.0 - (0.95**10) ** 10


def local(
    hidden_in,
    target_rows,
    grads,
    master,
    first_moment,
    second_moment,
    ref_weight,
    lengths,
    boundaries,
):
    total = lax.psum(jnp.sum(grads * grads), ("rep", "tp", "fsdp"))
    clip = 1.0 / jnp.sqrt(total + 1e-06)
    scaled = clip * grads
    moment_one = 0.9 * first_moment + 0.1 * scaled
    moment_two = 0.95 * second_moment + 0.05 * scaled * scaled
    corrected = moment_one / first_fix / (jnp.sqrt(moment_two / second_fix) + 1e-08)
    master_new = master - 0.002 * (corrected + 0.1 * master)
    delta = (master_new - ref_weight.astype(jnp.float32)).astype(jnp.bfloat16)
    gathered = lax.all_gather(hidden_in, "tp", axis=1, tiled=True)
    proj = jnp.dot(
        gathered,
        lax.all_gather(delta, ("rep", "fsdp"), axis=0, tiled=True),
        preferred_element_type=jnp.float32,
    )
    partial_score = 0.05 * jnp.sum(proj * target_rows.astype(jnp.float32), axis=1)
    count = lengths.shape[0]
    seq_len = partial_score.shape[0] // count
    position = jnp.arange(seq_len, dtype=jnp.int32)
    step_of = jnp.sum(
        (position[None, :, None] >= boundaries[:, None, :]).astype(jnp.int32), axis=-1
    )
    live = position[None, :] < lengths[:, None]
    onehot = (
        (step_of[:, :, None] == jnp.arange(STEPS + 1, dtype=jnp.int32)[None, None, :])
        & live[:, :, None]
    ).astype(jnp.float32)
    full_score = lax.psum(partial_score, "tp")
    step_rewards = jnp.sum(full_score.reshape(count, seq_len)[:, :, None] * onehot, axis=1)
    return (step_rewards, master_new, moment_one, moment_two)


def solution(mesh):
    placed = (
        P(("rep", "fsdp"), "tp"),
        P(("rep", "fsdp"), "tp"),
        P(("rep", "fsdp"), "tp"),
        P(("rep", "fsdp"), "tp"),
        P(("rep", "fsdp"), "tp"),
        P(("rep", "fsdp"), "tp"),
        P(("rep", "fsdp"), "tp"),
        P(("rep", "fsdp")),
        P(("rep", "fsdp"), None),
    )
    return jax.shard_map(
        local,
        mesh=mesh,
        in_specs=placed,
        out_specs=(
            P(("rep", "fsdp"), None),
            P(("rep", "fsdp"), "tp"),
            P(("rep", "fsdp"), "tp"),
            P(("rep", "fsdp"), "tp"),
        ),
        check_vma=False,
    )
```

profile of v0, /device:TPU:1, one launch (start us, length us, event | category | flops | bytes accessed | tf_op | source)
XLA Modules:
  0.0 452.2 jit_solution(7272561254811946726)
XLA Ops:
  7.2 0.0 all-gather.3.cloned.1.call-start
  7.2 1.6 multiply_reduce_fusion
  8.8 106.1 %psum.14 = f32[]{:T(128)} all-reduce(f32[]{:T(128)} %multiply_reduce_fusion), channel_id=1, replica_groups=mesh['rep'=16,'tp'=8,'fsdp'=4] {'rep','tp','fsdp'}, use_global_device_ids=true, to_apply=%region_2.0 | all-reduce | flops 1 | bytes 8 | tf_op jit(solution)/shard_map/psum | solution.py:24
  115.6 2.2 subtract_convert_fusion
  117.8 0.0 all-gather.3.cloned.1.call-update
  117.8 0.0 all-gather.5.cloned.1.call-start
  117.9 0.7 all-gather.5.cloned.1.call-update
  118.6 1.6 copy.14
  120.9 0.7 convert_reduce_fusion
  121.6 87.1 %all-gather.3.cloned.1.call-done = bf16[5120,640]{1,0:T(8,128)(2,1)} async-done(((bf16[80,640]{1,0:T(8,128)(2,1)}), bf16[5120,640]{1,0:T(8,128)(2,1)}) %all-gather.3.cloned.1.call-update) | async-done | bytes 6553616 | tf_op jit(solution)/shard_map/all_gather | solution.py:35
  208.7 210.4 %all-gather.5.cloned.1.call-done = bf16[1024,5120]{1,0:T(8,128)(2,1)} async-done(((bf16[1024,640]{1,0:T(8,128)(2,1)}), bf16[1024,5120]{1,0:T(8,128)(2,1)}) %all-gather.5.cloned.1.call-update) | async-done | bytes 10485776 | tf_op jit(solution)/shard_map/all_gather | solution.py:32
  419.1 11.6 %fusion = f32[1024]{0:T(1024)S(1)} fusion(bf16[1024,640]{0,1:T(8,128)(2,1)S(1)} %copy.14, bf16[5120,640]{1,0:T(8,128)(2,1)} %all-gather.3.cloned.1.call-done, bf16[1024,5120]{1,0:T(8,128)(2,1)} %all-gather.5.cloned.1.call-done), kind=kOutput, calls=%fused_computation.1 | convolution fusion | flops 6712851456 | bytes 18354176 | tf_op jit(solution)/shard_map/dot_general | solution.py:33
  430.8 13.9 %psum.15 = f32[1024]{0:T(1024)S(1)} all-reduce(f32[1024]{0:T(1024)S(1)} %broadcast_multiply_fusion), channel_id=1, replica_groups=mesh['rep'=16,'tp'=8,'fsdp'=4] {'tp'}, use_global_device_ids=true, to_apply=%region_4.0 | all-reduce | flops 1024 | bytes 8192 | tf_op jit(solution)/shard_map/psum | solution.py:50
  444.7 0.7 fusion.2
  (2 shorter events, 0.0 us)
Async XLA Ops:
  7.2 201.5 %all-gather.3.cloned.1.call-start = ((), (), s32[]{:S(2)}) async-start(), calls=%async_computation | async-start | bytes 6656000 | tf_op jit(solution)/shard_map/all_gather | solution.py:35
  117.8 301.3 %all-gather.5.cloned.1.call-start = ((), (), s32[]{:S(2)}) async-start(), calls=%async_computation.1 | async-start | bytes 11796480 | tf_op jit(solution)/shard_map/all_gather | solution.py:32
Sparse Core Ops, SparseCore 0:
  118.0 90.6 all-gather.2
  210.8 208.2 all-gather.4
where the time goes:
time: 456 us; the launch traced here: 452 us
  waiting for transfers between devices  298 us (65%)
  blocking collectives  120 us (26%)
  between operations  15.4 us (3%)
  matrix products  11.6 us (3%)
  other arithmetic  5.26 us (1%)
    all_gather x1, waiting for transfers between devices, local(): gathered = lax.all_gather(hidden_in, 'tp', axis=1, tiled=True)  210 us
    psum x1, blocking collectives, local(): total = lax.psum(jnp.sum(grads * grads), ('rep', 'tp', 'fsdp'))  106 us
    all_gather x1, waiting for transfers between devices, local(): lax.all_gather(delta, ('rep', 'fsdp'), axis=0, tiled=True)  87.1 us
    psum x1, blocking collectives, local(): full_score = lax.psum(partial_score, 'tp')  13.9 us
    dot_general x1, matrix products, local(): jnp.dot(gathered, lax.all_gather(delta, ('rep', 'fsdp'), axis=0, tiled=Tr...  11.6 us
  transfers between devices with their start and end apart: 2, of which 2 were waited for; matrix products, arithmetic and copies ran while one was open for 1% of the time, Pallas kernels for 0%

commit v1 on v0

v1 whole, which is shorter than its diff:
```python
import functools

import jax
import jax.numpy as jnp
from jax import lax
from jax.experimental import pallas as pl
from jax.experimental.pallas import tpu as pltpu
from jax.sharding import PartitionSpec as P

MESH = pl.DeviceIdType.MESH
STEPS = 8
NX, NY, NZ = 4, 8, 4
UNIT = (0, 1, 3, 2)
HALF = ((0, 2), (1, 3))

first_fix = 1.0 - (0.9**10) ** 10
second_fix = 1.0 - (0.95**10) ** 10


def kernel(
    hidden, target, grads, master, first, second, refw, lengths, bounds,
    steps_out, master_out, first_out, second_out,
    hid, tgt, dlt, piece, g_v, ma_v, m1_v, m2_v, rw_v, mo_v, o1_v, o2_v,
    na, nb, nc, sums, score,
    local_sem, out_sem,
    na_s, na_r, nb_s, nb_r, nc_s, nc_r, su_s, su_r,
    x_s, x_r, t_s, t_r, z_s, z_r, y_s, y_r, c_s, c_r,
):
    rep, tp, z = lax.axis_index("rep"), lax.axis_index("tp"), lax.axis_index("fsdp")
    y, core = rep // 2, rep % 2
    x, zl = tp // 2, tp % 2
    nrep, ntp = 2 * NY, 2 * NX
    rows = piece.shape[0]
    tokens = hid.shape[1]
    chunk = tokens // 4
    is_source = zl == y % 2

    def remote(src, dst, send, recv, device):
        return pltpu.make_async_remote_copy(
            src_ref=src, dst_ref=dst, send_sem=send, recv_sem=recv,
            device_id=device, device_id_type=MESH,
        )

    loads = [
        pltpu.make_async_copy(a, b, local_sem.at[i])
        for i, (a, b) in enumerate((
            (grads, g_v),
            (hidden, hid.at[x]),
            (first, m1_v),
            (second, m2_v),
            (master, ma_v),
            (refw, rw_v),
            (target, tgt.at[zl]),
        ))
    ]
    for c in loads:
        c.start()

    barrier = pltpu.get_barrier_semaphore()

    def greet(device):
        pl.semaphore_signal(barrier, inc=1, device_id=device, device_id_type=MESH)

    for r in range(1, nrep):
        greet(((rep + r) % nrep, tp, z))
    for r in range(1, ntp):
        greet((rep, (tp + r) % ntp, z))
    for r in range(1, NZ):
        greet((rep, tp, (z + r) % NZ))
        greet((rep, x * 2 + 1 - zl, (z + r) % NZ))

    loads[0].wait()
    g = g_v[...]
    sq = g * g
    part = jnp.sum(jnp.sum(sq, axis=0, keepdims=True), axis=1, keepdims=True)
    na[tp] = jnp.broadcast_to(part, (8, 128))
    pl.semaphore_wait(barrier, nrep - 1 + ntp - 1 + 2 * (NZ - 1))

    def spread(buf, me, n, sends, recv, device_of):
        out = []
        for r in range(1, n):
            c = remote(buf.at[me], buf.at[me], sends.at[r - 1], recv, device_of((me + r) % n))
            c.start()
            out.append(c)
        return out

    def gather_wait(buf, n, sends, recv):
        part = buf.at[pl.ds(0, n - 1)]
        remote(part, part, sends.at[0], recv, (rep, tp, z)).wait_recv()

    pending = []
    pending += spread(na, tp, ntp, na_s, na_r, lambda j: (rep, j, z))

    gather_wait(na, ntp, na_s, na_r)
    nb[rep] = jnp.sum(na[...], axis=0)
    pending += spread(nb, rep, nrep, nb_s, nb_r, lambda j: (j, tp, z))

    xp = (rep, ((x + 1) % NX) * 2 + zl, z)
    xm = (rep, ((x + NX - 1) % NX) * 2 + zl, z)
    loads[1].wait()

    def x_copy(d, k, owner, c):
        ref = hid.at[owner, pl.ds(c * chunk, chunk)]
        return remote(ref, ref, x_s.at[d, k], x_r.at[d, k], (xp, xm)[d])

    for i in range(4):
        for d, c in ((0, i), (1, (i + 2) % 4)):
            copy = x_copy(d, c, x, c)
            copy.start()
            pending.append(copy)

    gather_wait(nb, nrep, nb_s, nb_r)
    nc[z] = jnp.sum(nb[...], axis=0)
    pending += spread(nc, z, NZ, nc_s, nc_r, lambda j: (rep, tp, j))
    for c in loads[2:]:
        c.wait()
    gather_wait(nc, NZ, nc_s, nc_r)
    total = jnp.sum(nc[...], axis=0)[0:1, 0:1]
    clip = 1.0 / jnp.sqrt(total + 1e-06)

    scaled = clip * g_v[...]
    moment_one = 0.9 * m1_v[...] + 0.1 * scaled
    moment_two = 0.95 * m2_v[...] + 0.05 * scaled * scaled
    corrected = moment_one / first_fix / (jnp.sqrt(moment_two / second_fix) + 1e-08)
    old = ma_v[...]
    master_new = old - 0.002 * (corrected + 0.1 * old)
    delta = (master_new - rw_v[...].astype(jnp.float32)).astype(jnp.bfloat16)
    piece[...] = delta
    mo_v[...] = master_new
    o1_v[...] = moment_one
    o2_v[...] = moment_two

    def at(z_o, core_o):
        return pl.ds(pl.multiple_of((core_o * NZ + z_o) * rows, 16), rows)

    @pl.when(is_source)
    def _():
        dlt[y // 2, zl, at(z, core)] = delta

    def z_copy(r):
        return remote(
            piece, dlt.at[y // 2, zl, at(z, core)], z_s.at[r], z_r.at[z, zl],
            (rep, x * 2 + y % 2, (z + r) % NZ),
        )

    @pl.when(jnp.logical_not(is_source))
    def _():
        z_copy(0).start()

    for r in (1, 3, 2):
        z_copy(r).start()

    outs = [
        pltpu.make_async_copy(a, b, out_sem.at[i])
        for i, (a, b) in enumerate(((mo_v, master_out), (o1_v, first_out), (o2_v, second_out)))
    ]
    for c in outs:
        c.start()

    def t_copy(owner, c):
        ref = tgt.at[owner, pl.ds(c * chunk, chunk)]
        return remote(ref, ref, t_s.at[c], t_r.at[c], (rep, x * 2 + 1 - zl, z))

    for c in range(4):
        copy = t_copy(zl, c)
        copy.start()
        pending.append(copy)

    def x_relay(i):
        x_copy(0, i, (x + NX - 1) % NX, i).wait_recv()
        x_copy(0, 4 + i, (x + NX - 1) % NX, i).start()
        x_copy(1, 2 + i, (x + 1) % NX, 2 + i).wait_recv()
        x_copy(1, 4 + i, (x + 1) % NX, 2 + i).start()

    yp = (((y + 1) % NY) * 2 + core, tp, z)
    ym = (((y + NY - 1) % NY) * 2 + core, tp, z)
    other = (rep + 1 - 2 * core, tp, z)

    def unit(y_o, u, core_o):
        return dlt.at[(y_o + 2 * NY) % NY // 2, :, at((z + UNIT[u]) % NZ, core_o)]

    def y_copy(d, k, y_o, u):
        ref = unit(y_o, u, core)
        return remote(ref, ref, y_s.at[d, k], y_r.at[d, k], (yp, ym)[d])

    def c_copy(y_o, u, core_o):
        a = (y_o + 2 * NY) % NY // 2
        ref = unit(y_o, u, core_o)
        return remote(ref, ref, c_s.at[a, u], c_r.at[a, u], other)

    def origin(source, d, k):
        far = (4 if source else 3) if k >= 4 else (2 if source else 1)
        u = k if k < 4 else (HALF[d][k - 4] if source else k - 4)
        return (y - far if d == 0 else y + far), u

    def take(source, d, k):
        y_o, u = origin(source, d, k)
        y_copy(d, k, y_o, u).wait_recv()
        if k < 4:
            y_copy(d, k + (4 if source else 0), y_o, u).start()
        elif not source and u in HALF[d]:
            y_copy(d, 4 + HALF[d].index(u), y_o, u).start()
        c_copy(y_o, u, core).start()

    @pl.when(is_source)
    def _():
        for u in range(4):
            z_o = (z + UNIT[u]) % NZ
            for b in range(2):
                ref = dlt.at[y // 2, b, at(z_o, core)]
                arrival = remote(ref, ref, z_s.at[0], z_r.at[z_o, b], (rep, tp, z))
                if u == 0:
                    pl.when(b != zl)(lambda a=arrival: a.wait_recv())
                else:
                    arrival.wait_recv()
            y_copy(0, u, y, u).start()
            y_copy(1, u, y, u).start()
            c_copy(y, u, core).start()
        for k in range(6):
            if k in (1, 3):
                x_relay(k // 2)
            take(True, 0, k)
            take(True, 1, k)

    @pl.when(jnp.logical_not(is_source))
    def _():
        for k in range(8):
            if k in (2, 4):
                x_relay(k // 2 - 1)
            take(False, 0, k)
            take(False, 1, k)

    for c in range(4):
        t_copy(1 - zl, c).wait_recv()
    for k in range(4):
        if k >= 2:
            x_copy(0, k, (x + NX - 1) % NX, k).wait_recv()
        if k < 2:
            x_copy(1, k, (x + 1) % NX, k).wait_recv()
    for k in range(4, 6):
        x_copy(0, k, (x + 2) % NX, k - 4).wait_recv()
        x_copy(1, k, (x + 2) % NX, k - 2).wait_recv()
    for a in range(NX):
        for u in range(4):
            c_copy(2 * a + zl, u, 1 - core).wait_recv()

    width = dlt.shape[-1]

    def tile(t, carry):
        at_t = pl.ds(pl.multiple_of(t * chunk, chunk), chunk)
        acc = jnp.zeros((chunk, 128), jnp.float32)
        for b in range(2):
            proj = jnp.zeros((chunk, width), jnp.float32)
            for a in range(NX):
                proj += jnp.dot(hid[a, at_t], dlt[a, b], preferred_element_type=jnp.float32)
            prod = proj * tgt[b, at_t].astype(jnp.float32)
            for j in range(width // 128):
                acc += prod[:, j * 128 : (j + 1) * 128]
        score[at_t] = acc
        return carry

    lax.fori_loop(0, 4, tile, 0)

    lane = lax.broadcasted_iota(jnp.int32, (1, 128), 1)
    low = jnp.zeros((1, 128), jnp.int32)
    high = jnp.where(lane == STEPS, lengths[0], jnp.zeros((1, 128), jnp.int32))
    for k in range(STEPS):
        low = jnp.where(lane == k + 1, bounds[0, k], low)
        high = jnp.where(lane == k, jnp.minimum(bounds[0, k], lengths[0]), high)
    pos = lax.broadcasted_iota(jnp.int32, (tokens, 128), 0)
    inside = (pos >= low) & (pos < high)
    line = jnp.sum(score[...], axis=1, keepdims=True)
    part = 0.05 * jnp.sum(jnp.where(inside, line, 0.0), axis=0, keepdims=True)
    sums[tp] = jnp.broadcast_to(part, (8, 128))
    pending += spread(sums, tp, ntp, su_s, su_r, lambda j: (rep, j, z))
    gather_wait(sums, ntp, su_s, su_r)
    steps_out[...] = jnp.sum(sums[...], axis=0)[0:1, 0 : STEPS + 1]

    for c in pending:
        c.wait_send()
    for i in range(2):
        x_copy(0, 4 + i, (x + NX - 1) % NX, i).wait_send()
        x_copy(1, 4 + i, (x + 1) % NX, 2 + i).wait_send()
    for r in range(1, 4):
        z_copy(r).wait_send()
    for a in range(NX):
        for u in range(4):
            c_copy(2 * a + zl, u, core).wait_send()
    for d in range(2):
        for k in range(6):
            y_copy(d, k, y, 0).wait_send()

    @pl.when(is_source)
    def _():
        for d in range(2):
            for k in range(6, 8):
                y_copy(d, k, y, 0).wait_send()

    @pl.when(jnp.logical_not(is_source))
    def _():
        z_copy(0).wait_send()

    for c in outs:
        c.wait()


def local(hidden_in, target_rows, grads, master, first_moment, second_moment, ref_weight, lengths, boundaries):
    tokens, width = hidden_in.shape
    rows = grads.shape[0]
    f32, bf16 = jnp.float32, jnp.bfloat16
    weight = jax.ShapeDtypeStruct(grads.shape, f32)
    dma, vmem = pltpu.SemaphoreType.DMA, pltpu.VMEM
    any_space = pl.BlockSpec(memory_space=pl.ANY)
    smem = pl.BlockSpec(memory_space=pltpu.SMEM)
    return tuple(
        pl.pallas_call(
            kernel,
            out_shape=(jax.ShapeDtypeStruct((1, STEPS + 1), f32), weight, weight, weight),
            in_specs=[any_space] * 7 + [smem] * 2,
            out_specs=(pl.BlockSpec(memory_space=pltpu.VMEM), any_space, any_space, any_space),
            scratch_shapes=[
                vmem((NX, tokens, width), bf16),
                vmem((2, tokens, width), bf16),
                vmem((NX, 2, 8 * rows, width), bf16),
                vmem((rows, width), bf16),
                *[vmem((rows, width), f32)] * 4,
                vmem((rows, width), bf16),
                *[vmem((rows, width), f32)] * 3,
                vmem((2 * NX, 8, 128), f32),
                vmem((2 * NY, 8, 128), f32),
                vmem((NZ, 8, 128), f32),
                vmem((2 * NX, 8, 128), f32),
                vmem((tokens, 128), f32),
                dma((7,)),
                dma((3,)),
                dma((2 * NX - 1,)), dma(()),
                dma((2 * NY - 1,)), dma(()),
                dma((NZ - 1,)), dma(()),
                dma((2 * NX - 1,)), dma(()),
                dma((2, 6)), dma((2, 6)),
                dma((4,)), dma((4,)),
                dma((4,)), dma((4, 2)),
                dma((2, 8)), dma((2, 8)),
                dma((4, 4)), dma((4, 4)),
            ],
            compiler_params=pltpu.CompilerParams(
                collective_id=0, has_side_effects=True, vmem_limit_bytes=48 * 2**20
            ),
            cost_estimate=pl.CostEstimate(
                flops=2 * tokens * 8 * width * width, bytes_accessed=6 * 2**20, transcendentals=0
            ),
        )(hidden_in, target_rows, grads, master, first_moment, second_moment, ref_weight, lengths, boundaries)
    )


def solution(mesh):
    block = P(("rep", "fsdp"), "tp")
    return jax.shard_map(
        local,
        mesh=mesh,
        in_specs=(block,) * 7 + (P(("rep", "fsdp")), P(("rep", "fsdp"), None)),
        out_specs=(P(("rep", "fsdp"), None), block, block, block),
        check_vma=False,
    )
```

time: 456 us -> 105 us (0.23)
  waiting for transfers between devices: 298 us -> 0 us
  blocking collectives: 120 us -> 0 us
  Pallas kernels: 0 us -> 93.3 us
  between operations: 15.4 us -> 1.31 us
  matrix products: 11.6 us -> 0 us
  local copies, waits for them, and re-layouts: 1.61 us -> 10.4 us
  other arithmetic: 5.26 us -> 0 us
    all_gather x2 -> x0, waiting for transfers between devices: 297 us -> none  [the longest x1 210 us: local(): gathered = lax.all_gather(hidden_in, 'tp', axis=1, tiled=True)]
    psum x2 -> x0, blocking collectives: 120 us -> none  [the longest x1 106 us: local(): total = lax.psum(jnp.sum(grads * grads), ('rep', 'tp', 'fsdp'))]
    pallas_call x0 -> x1, Pallas kernels: none -> 93.3 us  [local(): pl.pallas_call(kernel, out_shape=(jax.ShapeDtypeStruct((1, STEPS + 1), f3...]
    dot_general x1 -> x0, matrix products: 11.6 us -> none  [local(): jnp.dot(gathered, lax.all_gather(delta, ('rep', 'fsdp'), axis=0, tiled=Tr...]
    unnamed x1 -> x20, local copies, waits for them, and re-layouts: 1.61 us -> 10.4 us
  transfers between devices with their start and end apart: 2 -> 0, of which waited for: 2 -> 0; matrix products, arithmetic and copies ran while one was open for 1% -> 0% of each run, Pallas kernels for 0% -> 0%
where the time goes in v1:
time: 105 us
  Pallas kernels  93.3 us (89%)
  local copies, waits for them, and re-layouts  10.4 us (10%)
  between operations  1.31 us (1%)
    pallas_call x1, Pallas kernels, local(): pl.pallas_call(kernel, out_shape=(jax.ShapeDtypeStruct((1, STEPS + 1), f3...  93.3 us
    unnamed x20, local copies, waits for them, and re-layouts  10.4 us

profile of v1, /device:TPU:1, one launch (start us, length us, event | category | flops | bytes accessed | tf_op | source)
XLA Modules:
  0.0 105.0 jit_solution(9100591490350382082)
XLA Ops:
  1.3 0.0 copy-start
  1.3 1.3 %copy-done = bf16[1024,640]{1,0:T(8,128)(2,1)S(1)} copy-done((bf16[1024,640]{1,0:T(8,128)(2,1)S(1)}, bf16[1024,640]{1,0:T(8,128)(2,1)}, u32[]{:S(2)}) %copy-start) | copy-done | bytes 1310744
  2.6 0.0 copy-start.1
  2.6 1.3 %copy-done.1 = bf16[1024,640]{1,0:T(8,128)(2,1)S(1)} copy-done((bf16[1024,640]{1,0:T(8,128)(2,1)S(1)}, bf16[1024,640]{1,0:T(8,128)(2,1)}, u32[]{:S(2)}) %copy-start.1) | copy-done | bytes 1310744
  3.9 0.0 copy-start.2
  3.9 0.9 copy-done.2
  4.8 0.0 copy-start.3
  4.8 0.9 copy-done.3
  5.8 0.0 copy-start.4
  5.8 0.9 copy-done.4
  6.7 0.0 copy-start.5
  6.7 0.9 copy-done.5
  7.6 0.0 copy-start.6
  7.6 0.9 copy-done.6
  8.5 0.0 copy-start.7
  8.5 0.7 copy-done.7
  9.2 93.3 %shard_map.120 = (f32[1,9]{1,0:T(1,128)S(1)}, f32[80,640]{1,0:T(8,128)S(1)}, f32[80,640]{1,0:T(8,128)S(1)}, f32[80,640]{1,0:T(8,128)S(1)}) custom-call(bf16[1024,640]{1,0:T(8,128)(2,1)S(1)} %copy-done, bf16[1024,640]{1,0:T(8,128)(2,1)S(1)} %copy-done.1, f32[80,640]{1,0:T(8,128)S(1)} %copy-done.2, f32[80,640]{1,0:T(8,128)S(1)} %copy-done.3, ...), custom_call_target="tpu_custom_call" | custom-call | flops 6710886400 | bytes 6291456 | tf_op jit(solution)/shard_map/pallas_call | solution.py:316
  102.5 0.5 copy.18
  103.0 0.7 copy.19
  103.7 0.7 copy.20
  104.3 0.7 copy.21
Async XLA Ops:
  1.3 1.3 %copy-start = (bf16[1024,640]{1,0:T(8,128)(2,1)S(1)}, bf16[1024,640]{1,0:T(8,128)(2,1)}, u32[]{:S(2)}) copy-start(bf16[1024,640]{1,0:T(8,128)(2,1)} %hidden.1) | copy-start | bytes 3932164
  2.6 1.3 %copy-start.1 = (bf16[1024,640]{1,0:T(8,128)(2,1)S(1)}, bf16[1024,640]{1,0:T(8,128)(2,1)}, u32[]{:S(2)}) copy-start(bf16[1024,640]{1,0:T(8,128)(2,1)} %target.1) | copy-start | bytes 3932164
  3.9 0.9 copy-start.2
  4.8 0.9 copy-start.3
  5.8 0.9 copy-start.4
  6.7 0.9 copy-start.5
  7.6 0.9 copy-start.6
  8.5 0.7 copy-start.7

commit v2 on v0

v2 whole, which is shorter than its diff:
```python
import functools

import jax
import jax.numpy as jnp
from jax import lax
from jax.experimental import pallas as pl
from jax.experimental.pallas import tpu as pltpu
from jax.sharding import PartitionSpec as P

MESH = pl.DeviceIdType.MESH
STEPS = 8
NX, NY, NZ = 4, 8, 4
NEAR = ((0, 1, 2, 3), (0, 2, 3, 1))
FAR = ((0, 1, 2, 3), (1, 2, 0, 3))


first_fix = 1.0 - (0.9**10) ** 10
second_fix = 1.0 - (0.95**10) ** 10


def kernel(
    hidden, target, grads, master, first, second, refw, lengths, bounds,
    total_out, sums_out,
    hid, tgt, dlt, piece, g_v, ma_v, m1_v, m2_v, rw_v,
    na, nb, nc, sums, score,
    local_sem,
    na_s, na_r, nb_s, nb_r, nc_s, nc_r, su_s, su_r,
    x_s, x_r, t_s, t_r, z_s, z_r, y_s, y_r, c_s, c_r,
):
    rep, tp, z = lax.axis_index("rep"), lax.axis_index("tp"), lax.axis_index("fsdp")
    y, core = rep // 2, rep % 2
    x, zl = tp // 2, tp % 2
    ntp = 2 * NX
    rows = piece.shape[0]
    tokens = hid.shape[1]
    half = tokens // 2
    chunk = tokens // 4
    is_source = zl == y % 2
    not_source = jnp.logical_not(is_source)

    def remote(src, dst, send, recv, device):
        return pltpu.make_async_remote_copy(
            src_ref=src, dst_ref=dst, send_sem=send, recv_sem=recv,
            device_id=device, device_id_type=MESH,
        )

    width = piece.shape[1]

    def half_of(b):
        return pl.ds(pl.multiple_of(b * width, 128), width)

    loads = [
        pltpu.make_async_copy(a, b, local_sem.at[i])
        for i, (a, b) in enumerate((
            (grads, g_v),
            (hidden, hid.at[x]),
            (first, m1_v),
            (second, m2_v),
            (master, ma_v),
            (refw, rw_v),
            (target, tgt.at[:, half_of(zl)]),
        ))
    ]
    for c in loads:
        c.start()

    barrier = pltpu.get_barrier_semaphore()

    def in_tp(j):
        return rep, j, z

    def in_y(j):
        return j * 2 + core, tp, z

    def in_cz(j):
        return y * 2 + j // NZ, tp, j % NZ

    def greet(device):
        pl.semaphore_signal(barrier, inc=1, device_id=device, device_id_type=MESH)

    cz = core * NZ + z
    for r in range(1, 8):
        greet(in_tp((tp + r) % 8))
        greet(in_y((y + r) % 8))
        greet(in_cz((cz + r) % 8))
    for r in range(1, NZ):
        greet((rep, x * 2 + 1 - zl, (z + r) % NZ))

    loads[0].wait()
    g = g_v[...]
    part = jnp.sum(jnp.sum(g * g, axis=0, keepdims=True), axis=1, keepdims=True)
    na[tp, 0:1] = jnp.broadcast_to(part, (1, 128))
    pl.semaphore_wait(barrier, 3 * 7 + NZ - 1)

    def spread(buf, me, sends, recv, device_of):
        out = []
        row = buf.at[me, pl.ds(0, 1)]
        for r in range(1, 8):
            c = remote(row, row, sends.at[r - 1], recv, device_of((me + r) % 8))
            c.start()
            out.append(c)
        return out

    def gather(buf, sends, recv):
        part = buf.at[pl.ds(0, 7), pl.ds(0, 1)]
        remote(part, part, sends.at[0], recv, (rep, tp, z)).wait_recv()
        return jnp.sum(buf[:, 0:1, :], axis=0)

    xp = (rep, ((x + 1) % NX) * 2 + zl, z)
    xm = (rep, ((x + NX - 1) % NX) * 2 + zl, z)

    def x_copy(d, k, owner, c):
        ref = hid.at[owner, pl.ds(c * half, half)]
        return remote(ref, ref, x_s.at[d, k], x_r.at[d, k], (xp, xm)[d])

    def x_relay():
        x_copy(0, 0, (x + NX - 1) % NX, 0).wait_recv()
        x_copy(0, 2, (x + NX - 1) % NX, 0).start()
        x_copy(1, 0, (x + 1) % NX, 1).wait_recv()
        x_copy(1, 2, (x + 1) % NX, 1).start()

    def t_copy(owner):
        ref = tgt.at[:, half_of(owner)]
        return remote(ref, ref, t_s, t_r, (rep, x * 2 + 1 - zl, z))

    pending = []

    def start(copy):
        copy.start()
        pending.append(copy)

    pending += spread(na, tp, na_s, na_r, in_tp)
    nb[y, 0:1] = gather(na, na_s, na_r)
    pending += spread(nb, y, nb_s, nb_r, in_y)

    loads[1].wait()
    for i in range(2):
        start(x_copy(0, i, x, i))
        start(x_copy(1, i, x, 1 - i))

    nc[cz, 0:1] = gather(nb, nb_s, nb_r)
    pending += spread(nc, cz, nc_s, nc_r, in_cz)
    score[...] = jnp.zeros_like(score)
    for c in loads[2:]:
        c.wait()
    total = gather(nc, nc_s, nc_r)
    total_out[...] = total
    total = total[:, 0:1]
    clip = 1.0 / jnp.sqrt(total + 1e-06)

    scaled = clip * g_v[...]
    moment_one = 0.9 * m1_v[...] + 0.1 * scaled
    moment_two = 0.95 * m2_v[...] + 0.05 * scaled * scaled
    corrected = moment_one / first_fix / (jnp.sqrt(moment_two / second_fix) + 1e-08)
    old = ma_v[...]
    master_new = old - 0.002 * (corrected + 0.1 * old)
    delta = (master_new - rw_v[...].astype(jnp.float32)).astype(jnp.bfloat16)
    piece[...] = delta

    def at(z_o, core_o):
        return pl.ds(pl.multiple_of((core_o * NZ + z_o) * rows, 16), rows)

    z_of = (z, z + 1 - 2 * (z % 2), NZ - 1 - z, (z + 2) % NZ)

    def z_copy(u):
        return remote(
            piece, dlt.at[y // 2, at(z, core), half_of(zl)], z_s.at[u], z_r.at[z, zl],
            (rep, x * 2 + y % 2, z_of[u]),
        )

    yp = in_y((y + 1) % NY)
    ym = in_y((y + NY - 1) % NY)
    other = (rep + 1 - 2 * core, tp, z)

    def unit(y_o, u, core_o):
        return dlt.at[(y_o + 2 * NY) % NY // 2, at(z_of[u], core_o)]

    def y_copy(d, k, y_o, u):
        ref = unit(y_o, u, core)
        return remote(ref, ref, y_s.at[d, k], y_r.at[d, k], (yp, ym)[d])

    def c_copy(y_o, pair, core_o):
        a = (y_o + 2 * NY) % NY // 2
        low = (core_o * 2 + (z // 2 + pair) % 2) * 2 * rows
        ref = dlt.at[a, pl.ds(pl.multiple_of(low, 16), 2 * rows)]
        return remote(ref, ref, c_s.at[a, pair], c_r.at[a, pair], other)

    def across(d, y_o, seen):
        if len(seen) >= 2:
            pair = seen[-1] // 2
            if {2 * pair, 2 * pair + 1} <= set(seen):
                c_copy(y_o, pair, core).start()

    def origin(d, hops):
        return y - hops if d == 0 else y + hops

    base = jnp.where(is_source, y // 2, (y + NY - 1) % NY // 2)
    turn = jnp.where(is_source, 1, -1)

    def ready(a):
        for pair in range(2):
            c_copy(2 * a + zl, pair, 1 - core).wait_recv()
        away = (a - x + NX) % NX

        @pl.when(away == 3)
        def _():
            x_copy(0, 1, (x + NX - 1) % NX, 1).wait_recv()

        @pl.when(away == 1)
        def _():
            x_copy(1, 1, (x + 1) % NX, 0).wait_recv()

        @pl.when(away == 2)
        def _():
            x_copy(0, 2, (x + 2) % NX, 0).wait_recv()
            x_copy(1, 2, (x + 2) % NX, 1).wait_recv()

    def products(low, high):
        def one(p, carry):
            i, t = p // 4, p % 4
            step = jnp.where(i == 1, NX - turn, jnp.where(i == 2, NX + turn, jnp.where(i == 3, 2, 0)))
            a = (base + step) % NX
            pl.when(t == 0)(lambda: ready(a))
            at_t = pl.ds(pl.multiple_of(t * chunk, chunk), chunk)
            acc = score[at_t]
            proj = jnp.dot(hid[a, at_t], dlt[a], preferred_element_type=jnp.float32)
            prod = proj * tgt[at_t].astype(jnp.float32)
            for j in range(2 * width // 128):
                acc += prod[:, j * 128 : (j + 1) * 128]
            score[at_t] = acc
            return carry

        lax.fori_loop(low, high, one, 0)

    @pl.when(is_source)
    def _():
        for u in (1, 2, 3):
            z_copy(u).start()
        dlt[y // 2, at(z, core), half_of(zl)] = delta
        t_copy(zl).start()
        for u in range(4):
            for b in range(2):
                ref = dlt.at[y // 2, at(z_of[u], core), half_of(b)]
                arrival = remote(ref, ref, z_s.at[1], z_r.at[z_of[u], b], (rep, tp, z))
                if u == 0:
                    pl.when(b != zl)(lambda a=arrival: a.wait_recv())
                else:
                    arrival.wait_recv()
            y_copy(0, u, y, u).start()
            if u != 1:
                y_copy(1, NEAR[1].index(u), y, u).start()
        y_copy(1, 3, y, 1).start()
        for pair in range(2):
            c_copy(y, pair, core).start()
        seen = [[], []]
        for i in range(4):
            if i == 1:
                x_relay()
            for d in range(2):
                near = FAR[d][i]
                late = []
                while len(seen[d]) <= near:
                    k = len(seen[d])
                    y_copy(d, k, origin(d, 2), NEAR[d][k]).wait_recv()
                    seen[d].append(NEAR[d][k])
                    late.append(list(seen[d]))
                y_copy(d, 4 + i, origin(d, 2), NEAR[d][near]).start()
                for got in late:
                    across(d, origin(d, 2), got)
        t_copy(1 - zl).wait_recv()
        products(0, 4)
        for d in range(2):
            for k in (4, 5):
                y_copy(d, k, origin(d, 4), NEAR[d][FAR[d][k - 4]]).wait_recv()
            c_copy(origin(d, 4), d, core).start()
        products(4, 12)
        for d in range(2):
            for k in range(8):
                y_copy(d, k, y, 0).wait_send()

    @pl.when(not_source)
    def _():
        for u in range(4):
            z_copy(u).start()
        t_copy(zl).start()
        for k in range(8):
            if k == 2:
                x_relay()
            for d in range(2):
                order = NEAR[d] if k < 4 else [NEAR[d][n] for n in FAR[d]]
                y_o = origin(d, 1 if k < 4 else 3)
                y_copy(d, k, y_o, order[k % 4]).wait_recv()
                if k < 6:
                    y_copy(d, k, y_o, order[k % 4]).start()
                across(d, y_o, order[: k % 4 + 1])
            if k == 5:
                t_copy(1 - zl).wait_recv()
                products(0, 4)
            if k == 6:
                products(4, 8)
        for d in range(2):
            for k in range(6):
                y_copy(d, k, y, 0).wait_send()
        z_copy(0).wait_send()

    products(jnp.where(is_source, 12, 8), 16)

    lane = lax.broadcasted_iota(jnp.int32, (1, 128), 1)
    low = jnp.zeros((1, 128), jnp.int32)
    high = jnp.where(lane == STEPS, lengths[0], jnp.zeros((1, 128), jnp.int32))
    for k in range(STEPS):
        low = jnp.where(lane == k + 1, bounds[0, k], low)
        high = jnp.where(lane == k, jnp.minimum(bounds[0, k], lengths[0]), high)
    pos = lax.broadcasted_iota(jnp.int32, (tokens, 128), 0)
    inside = (pos >= low) & (pos < high)
    line = jnp.sum(score[...], axis=1, keepdims=True)
    sums[tp, 0:1] = 0.05 * jnp.sum(jnp.where(inside, line, 0.0), axis=0, keepdims=True)
    pending += spread(sums, tp, su_s, su_r, in_tp)
    sums_out[...] = gather(sums, su_s, su_r)

    for c in pending:
        c.wait_send()
    t_copy(zl).wait_send()
    x_copy(0, 2, (x + NX - 1) % NX, 0).wait_send()
    x_copy(1, 2, (x + 1) % NX, 1).wait_send()
    for u in (1, 2, 3):
        z_copy(u).wait_send()
    for a in range(NX):
        for pair in range(2):
            c_copy(2 * a + zl, pair, core).wait_send()


def finish(total, sums, grads, master, first, second, steps_out, master_out, first_out, second_out):
    clip = 1.0 / jnp.sqrt(total[:, 0:1] + 1e-06)
    scaled = clip * grads[...]
    moment_one = 0.9 * first[...] + 0.1 * scaled
    moment_two = 0.95 * second[...] + 0.05 * scaled * scaled
    corrected = moment_one / first_fix / (jnp.sqrt(moment_two / second_fix) + 1e-08)
    old = master[...]
    master_out[...] = old - 0.002 * (corrected + 0.1 * old)
    first_out[...] = moment_one
    second_out[...] = moment_two
    steps_out[...] = sums[:, 0 : STEPS + 1]


def local(hidden_in, target_rows, grads, master, first_moment, second_moment, ref_weight, lengths, boundaries):
    tokens, width = hidden_in.shape
    rows = grads.shape[0]
    f32, bf16 = jnp.float32, jnp.bfloat16
    weight = jax.ShapeDtypeStruct(grads.shape, f32)
    line = jax.ShapeDtypeStruct((1, 128), f32)
    dma, vmem = pltpu.SemaphoreType.DMA, pltpu.VMEM
    any_space = pl.BlockSpec(memory_space=pl.ANY)
    smem = pl.BlockSpec(memory_space=pltpu.SMEM)
    in_vmem = pl.BlockSpec(memory_space=pltpu.VMEM)
    total, sums = pl.pallas_call(
        kernel,
        out_shape=(line, line),
        in_specs=[any_space] * 7 + [smem] * 2,
        out_specs=(in_vmem, in_vmem),
        scratch_shapes=[
            vmem((NX, tokens, width), bf16),
            vmem((tokens, 2 * width), bf16),
            vmem((NX, 8 * rows, 2 * width), bf16),
            vmem((rows, width), bf16),
            *[vmem((rows, width), f32)] * 4,
            vmem((rows, width), bf16),
            *[vmem((8, 8, 128), f32)] * 4,
            vmem((tokens, 128), f32),
            dma((7,)),
            *[dma((7,)), dma(())] * 4,
            dma((2, 3)), dma((2, 3)),
            dma(()), dma(()),
            dma((4,)), dma((4, 2)),
            dma((2, 8)), dma((2, 8)),
            dma((4, 2)), dma((4, 2)),
        ],
        compiler_params=pltpu.CompilerParams(
            collective_id=0, has_side_effects=True, vmem_limit_bytes=63 * 2**20
        ),
        cost_estimate=pl.CostEstimate(
            flops=2 * tokens * 8 * width * width, bytes_accessed=6 * 2**20, transcendentals=0
        ),
    )(hidden_in, target_rows, grads, master, first_moment, second_moment, ref_weight, lengths, boundaries)
    return tuple(
        pl.pallas_call(
            finish,
            out_shape=(jax.ShapeDtypeStruct((1, STEPS + 1), f32), weight, weight, weight),
            in_specs=[in_vmem] * 6,
            out_specs=(in_vmem,) * 4,
        )(total, sums, grads, master, first_moment, second_moment)
    )


def solution(mesh):
    block = P(("rep", "fsdp"), "tp")
    return jax.shard_map(
        local,
        mesh=mesh,
        in_specs=(block,) * 7 + (P(("rep", "fsdp")), P(("rep", "fsdp"), None)),
        out_specs=(P(("rep", "fsdp"), None), block, block, block),
        check_vma=False,
    )
```

time: 456 us -> 88.8 us (0.19)
  waiting for transfers between devices: 298 us -> 0 us
  blocking collectives: 120 us -> 0 us
  Pallas kernels: 0 us -> 87.4 us
  between operations: 15.4 us -> 1.29 us
  matrix products: 11.6 us -> 0 us
  other arithmetic: 5.26 us -> 0 us
    all_gather x2 -> x0, waiting for transfers between devices: 297 us -> none  [the longest x1 210 us: local(): gathered = lax.all_gather(hidden_in, 'tp', axis=1, tiled=True)]
    psum x2 -> x0, blocking collectives: 120 us -> none  [the longest x1 106 us: local(): total = lax.psum(jnp.sum(grads * grads), ('rep', 'tp', 'fsdp'))]
    pallas_call x0 -> x2, Pallas kernels: none -> 87.4 us  [the longest x1 85.1 us: local(): pl.pallas_call(kernel, out_shape=(line, line), in_specs=[any_space] * 7 +...]
    dot_general x1 -> x0, matrix products: 11.6 us -> none  [local(): jnp.dot(gathered, lax.all_gather(delta, ('rep', 'fsdp'), axis=0, tiled=Tr...]
  transfers between devices with their start and end apart: 2 -> 0, of which waited for: 2 -> 0; matrix products, arithmetic and copies ran while one was open for 1% -> 0% of each run, Pallas kernels for 0% -> 0%
where the time goes in v2:
time: 88.8 us; the launch traced here: 88.7 us
  Pallas kernels  87.4 us (98%)
  between operations  1.29 us (1%)
    pallas_call x1, Pallas kernels, local(): pl.pallas_call(kernel, out_shape=(line, line), in_specs=[any_space] * 7 +...  85.1 us
    pallas_call x1, Pallas kernels, local(): pl.pallas_call(finish, out_shape=(jax.ShapeDtypeStruct((1, STEPS + 1), f3...  2.34 us

profile of v2, /device:TPU:1, one launch (start us, length us, event | category | flops | bytes accessed | tf_op | source)
XLA Modules:
  0.0 88.7 jit_solution(5724740546445195256)
XLA Ops:
  1.3 85.1 %shard_map.120 = (f32[1,128]{1,0:T(1,128)}, f32[1,128]{1,0:T(1,128)}) custom-call(bf16[1024,640]{1,0:T(8,128)(2,1)} %hidden.1, bf16[1024,640]{1,0:T(8,128)(2,1)} %target.1, f32[80,640]{1,0:T(8,128)} %grads.3, f32[80,640]{1,0:T(8,128)} %master.3, f32[80,640]{1,0:T(8,128)} %first.3, f32[80,640]{1,0:T(8,128)} %second.3, bf16[80,640]{1,0:T(8,128)(2,1)} %refw.1, ...), custom_call_target="tpu_custom_call" | custom-call | flops 6710886400 | bytes 6291456 | tf_op jit(solution)/shard_map/pallas_call | solution.py:356
  86.3 2.3 %shard_map.121 = (f32[1,9]{1,0:T(1,128)}, f32[80,640]{1,0:T(8,128)}, f32[80,640]{1,0:T(8,128)}, f32[80,640]{1,0:T(8,128)}) custom-call(f32[1,128]{1,0:T(1,128)} %get-tuple-element.6.total, f32[1,128]{1,0:T(1,128)} %get-tuple-element.7.sums, f32[80,640]{1,0:T(8,128)} %grads.3, f32[80,640]{1,0:T(8,128)} %master.3, f32[80,640]{1,0:T(8,128)} %first.3, ...), custom_call_target="tpu_custom_call" | custom-call | tf_op jit(solution)/shard_map/pallas_call | solution.py:386

commit v3 on v2

--- a/solution.py
+++ b/solution.py
@@ -119,9 +119,9 @@
         x_copy(1, 0, (x + 1) % NX, 1).wait_recv()
         x_copy(1, 2, (x + 1) % NX, 1).start()
 
-    def t_copy(owner):
-        ref = tgt.at[:, half_of(owner)]
-        return remote(ref, ref, t_s, t_r, (rep, x * 2 + 1 - zl, z))
+    def t_copy(owner, c):
+        ref = tgt.at[pl.ds(pl.multiple_of(c * chunk, 16), chunk), half_of(owner)]
+        return remote(ref, ref, t_s.at[c], t_r.at[c], (rep, x * 2 + 1 - zl, z))
 
     pending = []
 
@@ -130,6 +130,7 @@
         pending.append(copy)
 
     pending += spread(na, tp, na_s, na_r, in_tp)
+    loads[6].wait()
     nb[y, 0:1] = gather(na, na_s, na_r)
     pending += spread(nb, y, nb_s, nb_r, in_y)
 
@@ -141,7 +142,7 @@
     nc[cz, 0:1] = gather(nb, nb_s, nb_r)
     pending += spread(nc, cz, nc_s, nc_r, in_cz)
     score[...] = jnp.zeros_like(score)
-    for c in loads[2:]:
+    for c in loads[2:6]:
         c.wait()
     total = gather(nc, nc_s, nc_r)
     total_out[...] = total
@@ -215,29 +216,33 @@
             x_copy(0, 2, (x + 2) % NX, 0).wait_recv()
             x_copy(1, 2, (x + 2) % NX, 1).wait_recv()
 
-    def products(low, high):
-        def one(p, carry):
-            i, t = p // 4, p % 4
-            step = jnp.where(i == 1, NX - turn, jnp.where(i == 2, NX + turn, jnp.where(i == 3, 2, 0)))
-            a = (base + step) % NX
-            pl.when(t == 0)(lambda: ready(a))
+    def products(pair):
+        a0, a1 = (base, (base + NX - turn) % NX) if pair == 0 else ((base + NX + turn) % NX, (base + 2) % NX)
+        ready(a0)
+        ready(a1)
+
+        def one(t, carry):
+            if pair == 0:
+                t_copy(1 - zl, t).wait_recv()
             at_t = pl.ds(pl.multiple_of(t * chunk, chunk), chunk)
+            proj = jnp.dot(hid[a0, at_t], dlt[a0], preferred_element_type=jnp.float32)
+            proj += jnp.dot(hid[a1, at_t], dlt[a1], preferred_element_type=jnp.float32)
+            prod = proj * tgt[at_t].astype(jnp.float32)
             acc = score[at_t]
-            proj = jnp.dot(hid[a, at_t], dlt[a], preferred_element_type=jnp.float32)
-            prod = proj * tgt[at_t].astype(jnp.float32)
             for j in range(2 * width // 128):
                 acc += prod[:, j * 128 : (j + 1) * 128]
             score[at_t] = acc
             return carry
 
-        lax.fori_loop(low, high, one, 0)
+        lax.fori_loop(0, 4, one, 0, unroll=2)
 
     @pl.when(is_source)
     def _():
         for u in (1, 2, 3):
             z_copy(u).start()
         dlt[y // 2, at(z, core), half_of(zl)] = delta
-        t_copy(zl).start()
+        for c in range(4):
+            t_copy(zl, c).start()
         for u in range(4):
             for b in range(2):
                 ref = dlt.at[y // 2, at(z_of[u], core), half_of(b)]
@@ -267,13 +272,11 @@
                 y_copy(d, 4 + i, origin(d, 2), NEAR[d][near]).start()
                 for got in late:
                     across(d, origin(d, 2), got)
-        t_copy(1 - zl).wait_recv()
-        products(0, 4)
+        products(0)
         for d in range(2):
             for k in (4, 5):
                 y_copy(d, k, origin(d, 4), NEAR[d][FAR[d][k - 4]]).wait_recv()
             c_copy(origin(d, 4), d, core).start()
-        products(4, 12)
         for d in range(2):
             for k in range(8):
                 y_copy(d, k, y, 0).wait_send()
@@ -282,7 +285,8 @@
     def _():
         for u in range(4):
             z_copy(u).start()
-        t_copy(zl).start()
+        for c in range(4):
+            t_copy(zl, c).start()
         for k in range(8):
             if k == 2:
                 x_relay()
@@ -294,16 +298,13 @@
                     y_copy(d, k, y_o, order[k % 4]).start()
                 across(d, y_o, order[: k % 4 + 1])
             if k == 5:
-                t_copy(1 - zl).wait_recv()
-                products(0, 4)
-            if k == 6:
-                products(4, 8)
+                products(0)
         for d in range(2):
             for k in range(6):
                 y_copy(d, k, y, 0).wait_send()
         z_copy(0).wait_send()
 
-    products(jnp.where(is_source, 12, 8), 16)
+    products(1)
 
     lane = lax.broadcasted_iota(jnp.int32, (1, 128), 1)
     low = jnp.zeros((1, 128), jnp.int32)
@@ -320,7 +321,8 @@
 
     for c in pending:
         c.wait_send()
-    t_copy(zl).wait_send()
+    for c in range(4):
+        t_copy(zl, c).wait_send()
     x_copy(0, 2, (x + NX - 1) % NX, 0).wait_send()
     x_copy(1, 2, (x + 1) % NX, 1).wait_send()
     for u in (1, 2, 3):
@@ -370,7 +372,7 @@
             dma((7,)),
             *[dma((7,)), dma(())] * 4,
             dma((2, 3)), dma((2, 3)),
-            dma(()), dma(()),
+            dma((4,)), dma((4,)),
             dma((4,)), dma((4, 2)),
             dma((2, 8)), dma((2, 8)),
             dma((4, 2)), dma((4, 2)),

time: 88.8 us -> 87.8 us (0.989)
  Pallas kernels: 87.4 us -> 86.4 us
    pallas_call x1, Pallas kernels: 85.1 us -> 84 us  [local(): pl.pallas_call(kernel, out_shape=(line, line), in_specs=[any_space] * 7 +...]
where the time goes in v3:
time: 87.8 us; the launch traced here: 87.7 us
  Pallas kernels  86.4 us (98%)
  between operations  1.29 us (1%)
    pallas_call x1, Pallas kernels, local(): pl.pallas_call(kernel, out_shape=(line, line), in_specs=[any_space] * 7 +...  84 us
    pallas_call x1, Pallas kernels, local(): pl.pallas_call(finish, out_shape=(jax.ShapeDtypeStruct((1, STEPS + 1), f3...  2.34 us

profile of v3, /device:TPU:1, one launch (start us, length us, event | category | flops | bytes accessed | tf_op | source)
XLA Modules:
  0.0 87.7 jit_solution(5033926952901477601)
XLA Ops:
  1.3 84.0 %shard_map.120 = (f32[1,128]{1,0:T(1,128)}, f32[1,128]{1,0:T(1,128)}) custom-call(bf16[1024,640]{1,0:T(8,128)(2,1)} %hidden.1, bf16[1024,640]{1,0:T(8,128)(2,1)} %target.1, f32[80,640]{1,0:T(8,128)} %grads.3, f32[80,640]{1,0:T(8,128)} %master.3, f32[80,640]{1,0:T(8,128)} %first.3, f32[80,640]{1,0:T(8,128)} %second.3, bf16[80,640]{1,0:T(8,128)(2,1)} %refw.1, ...), custom_call_target="tpu_custom_call" | custom-call | flops 6710886400 | bytes 6291456 | tf_op jit(solution)/shard_map/pallas_call | solution.py:358
  85.3 2.3 %shard_map.121 = (f32[1,9]{1,0:T(1,128)}, f32[80,640]{1,0:T(8,128)}, f32[80,640]{1,0:T(8,128)}, f32[80,640]{1,0:T(8,128)}) custom-call(f32[1,128]{1,0:T(1,128)} %get-tuple-element.6.total, f32[1,128]{1,0:T(1,128)} %get-tuple-element.7.sums, f32[80,640]{1,0:T(8,128)} %grads.3, f32[80,640]{1,0:T(8,128)} %master.3, f32[80,640]{1,0:T(8,128)} %first.3, ...), custom_call_target="tpu_custom_call" | custom-call | tf_op jit(solution)/shard_map/pallas_call | solution.py:388

commit v4 on v3

--- a/solution.py
+++ b/solution.py
@@ -316,8 +316,7 @@
     inside = (pos >= low) & (pos < high)
     line = jnp.sum(score[...], axis=1, keepdims=True)
     sums[tp, 0:1] = 0.05 * jnp.sum(jnp.where(inside, line, 0.0), axis=0, keepdims=True)
-    pending += spread(sums, tp, su_s, su_r, in_tp)
-    sums_out[...] = gather(sums, su_s, su_r)
+    last = spread(sums, tp, su_s, su_r, in_tp)
 
     for c in pending:
         c.wait_send()
@@ -330,6 +329,9 @@
     for a in range(NX):
         for pair in range(2):
             c_copy(2 * a + zl, pair, core).wait_send()
+    sums_out[...] = gather(sums, su_s, su_r)
+    for c in last:
+        c.wait_send()
 
 
 def finish(total, sums, grads, master, first, second, steps_out, master_out, first_out, second_out):

time: 87.8 us -> 87.7 us (level)
  no operation moved by 1% of the time
where the time goes in v4:
time: 87.7 us; the launch traced here: 87.6 us
  Pallas kernels  86.3 us (98%)
  between operations  1.29 us (1%)
    pallas_call x1, Pallas kernels, local(): pl.pallas_call(kernel, out_shape=(line, line), in_specs=[any_space] * 7 +...  83.9 us
    pallas_call x1, Pallas kernels, local(): pl.pallas_call(finish, out_shape=(jax.ShapeDtypeStruct((1, STEPS + 1), f3...  2.34 us

profile of v4, /device:TPU:1, one launch (start us, length us, event | category | flops | bytes accessed | tf_op | source)
XLA Modules:
  0.0 87.6 jit_solution(16808677788930274097)
XLA Ops:
  1.3 83.9 %shard_map.120 = (f32[1,128]{1,0:T(1,128)}, f32[1,128]{1,0:T(1,128)}) custom-call(bf16[1024,640]{1,0:T(8,128)(2,1)} %hidden.1, bf16[1024,640]{1,0:T(8,128)(2,1)} %target.1, f32[80,640]{1,0:T(8,128)} %grads.3, f32[80,640]{1,0:T(8,128)} %master.3, f32[80,640]{1,0:T(8,128)} %first.3, f32[80,640]{1,0:T(8,128)} %second.3, bf16[80,640]{1,0:T(8,128)(2,1)} %refw.1, ...), custom_call_target="tpu_custom_call" | custom-call | flops 6710886400 | bytes 6291456 | tf_op jit(solution)/shard_map/pallas_call | solution.py:360
  85.2 2.3 %shard_map.121 = (f32[1,9]{1,0:T(1,128)}, f32[80,640]{1,0:T(8,128)}, f32[80,640]{1,0:T(8,128)}, f32[80,640]{1,0:T(8,128)}) custom-call(f32[1,128]{1,0:T(1,128)} %get-tuple-element.6.total, f32[1,128]{1,0:T(1,128)} %get-tuple-element.7.sums, f32[80,640]{1,0:T(8,128)} %grads.3, f32[80,640]{1,0:T(8,128)} %master.3, f32[80,640]{1,0:T(8,128)} %first.3, ...), custom_call_target="tpu_custom_call" | custom-call | tf_op jit(solution)/shard_map/pallas_call | solution.py:390
